TPU v7x, 32 devices: a whole 2x2x4 slice. The times are simulated.
32 devices in a mesh: rows: 8 (over y, x, core), lags: 4 (over z).
Axes of the slice: x: 2, y: 2, z: 4, core: 2. Of those that a mesh axis runs over, the one named last changes fastest.
Arguments:
- history: float32 [32, 16, 2048], P('lags', None, 'rows'), may hold values from -6 to 6
- incident: float32 [2, 16, 2048], P(None, None, 'rows'), may hold values from -6 to 6
- kernel: float32 [8, 32, 6, 256, 256], P('rows', 'lags'), may hold values from -0.02734375 to 0.02734375
- near_blocks: int32 [8, 32, 6], P('rows', 'lags'), may hold values from 0 to 7, as said below
- self_inverse: float32 [8, 256, 256], P('rows'), may hold values from -1 to 1
Outputs:
- densities: float32 [2, 16, 2048], P(None, None, 'rows')
Inputs may be any that keep to these rules, and one draw needn't show every extreme that they name: `near_blocks`: indices of source blocks; for each row block and each group of 8 consecutive lags, no source block appears more than 6 times among its 48 entries, and some block appears exactly 6 times.
All inputs are finite; a program needn't handle non-finite values.
Results may differ from a plain program's by a relative error of at most 0.00012.
Values sent between devices are 32-bit elements; how exact they have to be, the bound alone decides.
A program may use at most 128 MiB of HBM per device.

v0:
```python
import jax
import jax.numpy as jnp
from jax import lax
from jax.sharding import PartitionSpec as P


def shifted(block, axis, distance):
    devices = range(lax.axis_size(axis))
    route = [(i - distance, i) for i in devices if i - distance in devices]
    return lax.ppermute(block, axis, route)


def shards(history, incident, kernel, near_blocks, self_inverse):
    highest = lax.Precision.HIGHEST
    lag_dev, wave_count, block_size = history.shape
    step_count = incident.shape[0]
    lag_group = lax.axis_index("lags")
    kernel_rows = kernel[0]
    source_ids = near_blocks[0]
    near_count = source_ids.shape[1]
    inverse = self_inverse[0]
    lag_ids = jnp.arange(lag_dev, dtype=jnp.int32)

    def solve_from(instant, picked):
        partial_value = jnp.einsum("jkwc,jkcr->wr", picked, kernel_rows, precision=highest)
        driving = lax.dynamic_index_in_dim(incident, instant, 0, keepdims=False)
        near_field = lax.psum(partial_value, "lags")
        result = jnp.dot(
            driving - near_field, inverse, precision=highest, preferred_element_type=jnp.float32
        )
        return result

    outputs = jnp.zeros((step_count, wave_count, block_size), jnp.float32)
    all_near = lax.all_gather(near_blocks, "rows", axis=0, tiled=True)
    block_count = all_near.shape[0]
    slot_total = lag_dev * near_count
    most_times = max(1, (slot_total + block_count - 1) // block_count)
    row_index = lax.axis_index("rows")
    flat_near = all_near.reshape(block_count, slot_total)
    matching = flat_near == row_index
    ranking = jnp.cumsum(matching.astype(jnp.int32), axis=1) - 1
    slot_range = jnp.arange(most_times, dtype=jnp.int32)
    chosen = matching[:, None, :] & (ranking[:, None, :] == slot_range[None, :, None])
    chosen_lag = (
        chosen.astype(jnp.float32).reshape(block_count, most_times, lag_dev, near_count).sum(axis=3)
    )
    own_list = source_ids.reshape(slot_total)
    positions = jnp.arange(slot_total, dtype=jnp.int32)
    earlier = (own_list[:, None] == own_list[None, :]) & (positions[None, :] < positions[:, None])
    own_rank = jnp.sum(earlier.astype(jnp.int32), axis=1)
    flat_index = own_list * most_times + own_rank

    def fetch_and_solve(instant, window):
        slot_ids = jnp.remainder(lag_ids - instant, lag_dev)
        ordered = window[slot_ids]
        outgoing = jnp.einsum("rcj,jwb->rcwb", chosen_lag, ordered, precision=highest)
        arrived = lax.all_to_all(outgoing, "rows", split_axis=0, concat_axis=0, tiled=True)
        flat_arrived = arrived.reshape(block_count * most_times, wave_count, block_size)
        picked = flat_arrived[flat_index].reshape(lag_dev, near_count, wave_count, block_size)
        return solve_from(instant, picked)

    def march(instant, state_tuple):
        window, results = state_tuple
        density = fetch_and_solve(instant, window)
        results = lax.dynamic_update_index_in_dim(results, density, instant, 0)
        free_slot = jnp.remainder(lag_dev - 1 - instant, lag_dev)
        leaving = lax.dynamic_index_in_dim(window, free_slot, 0, keepdims=False)
        passed = shifted(leaving, "lags", 1)
        entering_local = jnp.where(lag_group == 0, density, passed)
        window = lax.dynamic_update_index_in_dim(window, entering_local, free_slot, 0)
        return (window, results)

    window, outputs = lax.fori_loop(0, step_count - 1, march, (history, outputs))
    last_density = fetch_and_solve(step_count - 1, window)
    outputs = lax.dynamic_update_index_in_dim(outputs, last_density, step_count - 1, 0)
    return outputs


def solution(mesh):
    in_specs = (
        P("lags", None, "rows"),
        P(None, None, "rows"),
        P("rows", "lags", None, None, None),
        P("rows", "lags", None),
        P("rows", None, None),
    )
    out_specs = P(None, None, "rows")
    return jax.shard_map(shards, mesh=mesh, in_specs=in_specs, out_specs=out_specs, check_vma=False)
```

profile of v0, /device:TPU:0, one launch (start us, length us, event | category | flops | bytes accessed | tf_op | source)
XLA Modules:
  0.0 103.4 jit_solution(9371490613631375984)
XLA Ops:
  0.0 0.0 copy-start
  0.0 0.0 copy-start.1
  0.0 0.9 copy.48
  1.0 0.8 copy.26
  1.7 10.5 %all_gather.3 = s32[8,8,6]{2,1,0:T(8,128)S(1)} all-gather(s32[1,8,6]{2,1,0:T(8,128)S(1)} %copy.26), channel_id=1, replica_groups=mesh['rows'=8,'lags'=4] {'rows'}, dimensions={0}, use_global_device_ids=true | all-gather | bytes 1728 | tf_op jit(solution)/shard_map/all_gather | solution.py:34
  12.2 0.1 reshape.158
  12.3 0.2 reduce_window_sum.11
  12.5 0.1 sub.25
  12.6 0.1 copy.28
  12.7 0.1 copy.27
  12.9 0.6 gather_fusion
  13.5 0.8 fusion.16
  14.3 1.1 %copy.30 = f32[8,6,16,256]{3,2,1,0:T(8,128)} copy(f32[8,6,16,256]{3,0,2,1:T(8,128)S(1)} %fusion.16) | data formatting | bytes 1572864 | tf_op jit(solution)/shard_map/while/body/eval_jaxpr/rcj,jwb->rcwb/dot_general | solution.py:56
  15.4 3.5 %all-to-all-start = ((f32[8,6,16,256]{3,2,1,0:T(8,128)}), f32[8,6,16,256]{3,2,1,0:T(8,128)S(1)}, u32[]{:S(2)}, u32[]{:S(2)}) async-start(f32[8,6,16,256]{3,2,1,0:T(8,128)} %copy.30), calls=%async_computation | async-start | bytes 1572864 | tf_op jit(solution)/shard_map/while/body/eval_jaxpr/all_to_all | solution.py:57
  18.9 3.5 %collective-permute-start = (f32[16,256]{1,0:T(8,128)S(1)}, f32[16,256]{1,0:T(8,128)S(1)}, u32[]{:S(2)}, u32[]{:S(2)}) collective-permute-start(f32[16,256]{1,0:T(8,128)S(1)} %slice_bitcast_fusion), channel_id=1, source_target_pairs={{0,1},{1,2},{2,3},{4,5},{5,6},{6,7},{8,9},{9,10},{10,11},{12,13},{... | collective-permute-start | bytes 49160 | tf_op jit(solution)/shard_map/while/body/eval_jaxpr/ppermute | solution.py:10
  22.5 0.7 broadcast_multiply_fusion
  23.1 0.1 eq.60
  23.2 0.1 copy.31
  23.3 0.1 mul.18
  23.4 0.2 convert_reduce_fusion.1
  23.6 7.8 %all-to-all-done = f32[8,6,16,256]{3,2,1,0:T(8,128)S(1)} async-done(((f32[8,6,16,256]{3,2,1,0:T(8,128)}), f32[8,6,16,256]{3,2,1,0:T(8,128)S(1)}, u32[]{:S(2)}, u32[]{:S(2)}) %all-to-all-start) | async-done | bytes 786464 | tf_op jit(solution)/shard_map/while/body/eval_jaxpr/all_to_all | solution.py:57
  31.5 0.6 gather_fusion.1
  32.1 9.2 %fusion.4 = f32[16,256]{1,0:T(8,128)S(1)} fusion(f32[8,6,16,256]{3,2,1,0:T(8,128)S(1)} %bitcast.71, f32[1,8,6,256,256]{4,3,2,1,0:T(8,128)} %param.7), kind=kOutput, calls=%fused_computation.8 | convolution fusion | flops 603979776 | bytes 13385728 | tf_op jit(solution)/shard_map/while/body/eval_jaxpr/jkwc,jkcr->wr/dot_general | solution.py:25
  41.3 19.0 %psum.15 = f32[16,256]{1,0:T(8,128)S(1)} all-reduce(f32[16,256]{1,0:T(8,128)S(1)} %fusion.4), channel_id=1, replica_groups=mesh['rows'=8,'lags'=4] {'lags'}, use_global_device_ids=true, to_apply=%region_3.4 | all-reduce | flops 4096 | bytes 32768 | tf_op jit(solution)/shard_map/while/body/eval_jaxpr/psum | solution.py:27
  60.3 0.0 collective-permute-done
  60.3 0.0 copy-done
  60.3 0.0 copy-done.1
  60.3 0.2 bitcast_dynamic-update-slice_fusion
  60.5 0.6 gather_fusion.2
  61.1 0.8 fusion.14
  61.9 0.3 copy.34
  62.2 15.0 %all_to_all.11 = f32[8,6,16,256]{3,2,1,0:T(8,128)S(1)} all-to-all(f32[8,6,16,256]{3,2,1,0:T(8,128)S(1)} %copy.34), channel_id=1, replica_groups=mesh['rows'=8,'lags'=4] {'rows'}, dimensions={0} | all-to-all | bytes 1572864 | tf_op jit(solution)/shard_map/all_to_all | solution.py:57
  77.1 0.6 gather_fusion.3
  77.7 9.2 %fusion.7 = f32[16,256]{1,0:T(8,128)S(1)} fusion(f32[8,6,16,256]{3,2,1,0:T(8,128)S(1)} %bitcast.70, f32[1,8,6,256,256]{4,3,2,1,0:T(8,128)} %param.7), kind=kOutput, calls=%fused_computation.9 | convolution fusion | flops 603979776 | bytes 13385728 | tf_op jit(solution)/shard_map/jkwc,jkcr->wr/dot_general | solution.py:25
  87.0 15.6 %psum.16 = f32[16,256]{1,0:T(8,128)S(1)} all-reduce(f32[16,256]{1,0:T(8,128)S(1)} %fusion.7), channel_id=1, replica_groups=mesh['rows'=8,'lags'=4] {'lags'}, use_global_device_ids=true, to_apply=%region_4.5 | all-reduce | flops 4096 | bytes 32768 | tf_op jit(solution)/shard_map/psum | solution.py:27
  102.5 0.2 convolution_bitcast_fusion
  102.7 0.6 pad_maximum_fusion
  (10 shorter events, 0.1 us)
Async XLA Ops:
  0.0 60.3 %copy-start = (f32[1,256,256]{2,1,0:T(8,128)S(1)}, f32[1,256,256]{2,1,0:T(8,128)}, u32[]{:S(2)}) copy-start(f32[1,256,256]{2,1,0:T(8,128)} %param.9) | copy-start | bytes 786436
  0.0 60.3 %copy-start.1 = (f32[2,16,256]{2,1,0:T(8,128)S(1)}, f32[2,16,256]{2,1,0:T(8,128)}, u32[]{:S(2)}) copy-start(f32[2,16,256]{2,1,0:T(8,128)} %param.6) | copy-start | bytes 98308
  15.4 16.1 %all-to-all-start = ((f32[8,6,16,256]{3,2,1,0:T(8,128)}), f32[8,6,16,256]{3,2,1,0:T(8,128)S(1)}, u32[]{:S(2)}, u32[]{:S(2)}) async-start(f32[8,6,16,256]{3,2,1,0:T(8,128)} %copy.30), calls=%async_computation | async-start | bytes 1572864 | tf_op jit(solution)/shard_map/while/body/eval_jaxpr/all_to_all | solution.py:57
  18.9 41.4 %collective-permute-start = (f32[16,256]{1,0:T(8,128)S(1)}, f32[16,256]{1,0:T(8,128)S(1)}, u32[]{:S(2)}, u32[]{:S(2)}) collective-permute-start(f32[16,256]{1,0:T(8,128)S(1)} %slice_bitcast_fusion), channel_id=1, source_target_pairs={{0,1},{1,2},{2,3},{4,5},{5,6},{6,7},{8,9},{9,10},{10,11},{12,13},{... | collective-permute-start | bytes 49160 | tf_op jit(solution)/shard_map/while/body/eval_jaxpr/ppermute | solution.py:10
where the time goes:
time: 104 us; the launch traced here: 103 us
  blocking collectives  60 us (58%)
  matrix products  20.4 us (20%)
  waiting for transfers between devices  7.84 us (8%)
  starting transfers between devices  7.05 us (7%)
  local copies, waits for them, and re-layouts  6.1 us (6%)
  other arithmetic  1.82 us (2%)
    psum x2, blocking collectives, solve_from(): near_field = lax.psum(partial_value, 'lags')  34.6 us
    dot_general x2, matrix products, solve_from(): jnp.einsum('jkwc,jkcr->wr', picked, kernel_rows, precision=highest)  18.4 us
    all_to_all x1, blocking collectives, fetch_and_solve(): lax.all_to_all(outgoing, 'rows', split_axis=0, concat_axis=0, tiled=True)  15 us
    all_gather x1, blocking collectives, shards(): all_near = lax.all_gather(near_blocks, 'rows', axis=0, tiled=True)  10.5 us
    all_to_all x1, waiting for transfers between devices, fetch_and_solve(): lax.all_to_all(outgoing, 'rows', split_axis=0, concat_axis=0, tiled=True)  7.84 us
    all_to_all x1, starting transfers between devices, fetch_and_solve(): lax.all_to_all(outgoing, 'rows', split_axis=0, concat_axis=0, tiled=True)  3.55 us
    ppermute x1, starting transfers between devices, shifted(): return lax.ppermute(block, axis, route)  3.51 us
  transfers between devices with their start and end apart: 2, of which 1 were waited for; matrix products, arithmetic and copies ran while one was open for 11% of the time, Pallas kernels for 0%

commit v1 on v0

v1 whole, which is shorter than its diff:
```python
import functools

import jax
import jax.numpy as jnp
from jax import lax
from jax.experimental import pallas as pl
from jax.experimental.pallas import tpu as pltpu
from jax.sharding import PartitionSpec as P

MESH = pl.DeviceIdType.MESH
VMEM_LIMIT = 58 * 1024 * 1024


def split(x):
    high = x.astype(jnp.bfloat16)
    low = (x - high.astype(jnp.float32)).astype(jnp.bfloat16)
    return high, low


def product(x, high, low):
    m = x.shape[0]
    xh, xl = split(x)
    both = jnp.dot(jnp.concatenate([xh, xl], 0), high, preferred_element_type=jnp.float32)
    rest = jnp.dot(xh, low, preferred_element_type=jnp.float32)
    return both[:m] + (both[m:] + rest)


def march(
    rows, groups, per_chunk,
    near, hist, inc_hbm, ker, inv_hbm, out,
    kbuf, khigh, klow, extra, acc, part, dens, inc, inv, ihigh, ilow,
    ker_sem, in_sem, own_sem, out_sem,
    send_sem, direct_sem, pass_send, pass_sem,
    extra_send, extra_sem, epass_send, epass_sem,
    part_send, part_sem, dens_send, dens_sem, res_send, res_sem,
    *past,
):
    lags, waves, block = hist.shape
    steps = inc_hbm.shape[0]
    slots = near.shape[0]
    ahead = steps - 1
    half = rows // 2
    chunks = lags // per_chunk
    row = lax.axis_index("rows")
    group = lax.axis_index("lags")
    core = lax.rem(row, 2)
    place = lax.div(row, 2)
    partner = row + 1 - 2 * core

    def remote(src, dst, send, recv, r, g):
        return pltpu.make_async_remote_copy(
            src_ref=src, dst_ref=dst, send_sem=send, recv_sem=recv,
            device_id=(r, g), device_id_type=MESH,
        )

    def all_of(ref, sem):
        pltpu.make_async_copy(ref, ref, sem).wait()

    def lags_of(c):
        return hist.at[pl.ds(c * per_chunk, per_chunk)]

    own = [
        pltpu.make_async_copy(lags_of(c), past[c].at[core, place], own_sem.at[c])
        for c in range(chunks)
    ]
    for copy in own:
        copy.start()
    loads = [pltpu.make_async_copy(ker.at[0, j], kbuf.at[j], ker_sem.at[j]) for j in range(lags)]
    inc_load = pltpu.make_async_copy(inc_hbm, inc, in_sem.at[0])
    inv_load = pltpu.make_async_copy(inv_hbm.at[0], inv, in_sem.at[1])

    barrier = pltpu.get_barrier_semaphore()

    def greet(r, g):
        pl.semaphore_signal(barrier, inc=1, device_id=(r, g), device_id_type=MESH)

    for m in range(1, rows):
        greet(lax.rem(row + m, rows), group)
    for m in range(1, groups):
        greet(row, lax.rem(group + m, groups))

    @pl.when(group > 0)
    def _():
        for m in range(1, half):
            greet(lax.rem(row + 2 * m, rows), group - 1)

    @pl.when(group < groups - 1)
    def _():
        for m in range(1, half):
            greet(lax.rem(row + 2 * m, rows), group + 1)

    for load in loads:
        load.start()
    inv_load.start()
    inc_load.start()

    sides = (group > 0).astype(jnp.int32) + (group < groups - 1).astype(jnp.int32)
    pl.semaphore_wait(barrier, rows - 1 + groups - 1 + (half - 1) * sides)

    def chunk_copy(c, m):
        return remote(
            lags_of(c), past[c].at[core, place],
            send_sem.at[c], direct_sem.at[c], lax.rem(row + 2 * m, rows), group,
        )

    def chunk_pass(c):
        ref = past[c].at[core]
        return remote(ref, ref, pass_send.at[c], pass_sem.at[c], partner, group)

    def extra_copy(m, g):
        return remote(
            hist.at[pl.ds(lags - ahead, ahead)], extra.at[core, place],
            extra_send, extra_sem, lax.rem(row + 2 * m, rows), g,
        )

    def extra_pass():
        ref = extra.at[core]
        return remote(ref, ref, epass_send, epass_sem, partner, group)

    for c in range(chunks):
        for m in range(1, half):
            chunk_copy(c, m).start()
        if c == 0 and ahead > 0:

            @pl.when(group < groups - 1)
            def _():
                for m in range(half):
                    extra_copy(m, group + 1).start()

    if ahead > 0:

        @pl.when(group == 0)
        def _():
            extra[...] = jnp.zeros(extra.shape, jnp.float32)

    def convert(j):
        loads[j].wait()

        @pl.loop(0, slots)
        def _(k):
            high, low = split(kbuf[j, k])
            at = pl.ds(pl.multiple_of(k * block, block), block)
            khigh[j, at] = high
            klow[j, at] = low

    def pass_on(c):
        own[c].wait()
        if half > 1:
            all_of(past[c].at[core, pl.ds(0, half - 1)], direct_sem.at[c])
        chunk_pass(c).start()

    def entry(h, b):
        at = (lax.rem(b, 2), lax.div(b, 2))
        if h < 0:
            return extra[at[0], at[1], h + ahead]
        return past[h // per_chunk][at[0], at[1], h % per_chunk]

    def multiply(c):
        chunk_pass(c).wait_recv()
        for j in range(c * per_chunk, (c + 1) * per_chunk):
            pieces = []
            for k in range(slots):
                b = near[k, 0, j]
                pieces.append(jnp.concatenate([entry(j - s, b) for s in range(ahead, -1, -1)], 0))
            value = product(jnp.concatenate(pieces, 1), khigh[j], klow[j])
            value = value.reshape(steps, waves, block)
            if j == 0:
                acc[...] = value
            else:
                acc[...] += value

    done = 0
    for c in range(chunks):
        for j in range(c * per_chunk, (c + 1) * per_chunk):
            convert(j)
        pass_on(c)
        if c == min(1, chunks - 1) and ahead > 0:

            @pl.when(group > 0)
            def _():
                all_of(extra.at[core], extra_sem)
                extra_pass().start()

        if c >= 2:
            if done == 0 and ahead > 0:

                @pl.when(group > 0)
                def _():
                    extra_pass().wait_recv()

            multiply(done)
            done += 1
    if done == 0 and ahead > 0:

        @pl.when(group > 0)
        def _():
            extra_pass().wait_recv()

    inv_load.wait()
    ihigh[...], ilow[...] = split(inv[...])
    for c in range(done, chunks):
        multiply(c)

    def part_copy(s, to):
        t = ahead - s
        return remote(acc.at[t], part.at[group, t], part_send.at[s], part_sem.at[s], row, to)

    def result_copy(s, g):
        return remote(dens.at[s, row], out.at[s], res_send.at[s], res_sem.at[s], row, g)

    def dens_copy(s, m):
        ref = dens.at[s, row]
        return remote(ref, ref, dens_send.at[s], dens_sem.at[s], lax.rem(row + m, rows), group)

    inc_load.wait()

    @pl.when(group > 0)
    def _():
        for s in range(steps):
            part_copy(s, 0).start()
        for s in range(steps):
            part_copy(s, 0).wait_send()
        for s in range(steps):
            result_copy(s, 0).wait_recv()

    @pl.when(group == 0)
    def _():
        def keep(s):
            return pltpu.make_async_copy(dens.at[s, row], out.at[s], out_sem.at[s])

        for s in range(steps):
            t = ahead - s
            all_of(part.at[pl.ds(0, groups - 1), t], part_sem.at[s])
            near_field = acc[t]
            for g in range(1, groups):
                near_field = near_field + part[g, t]
            if s > 0:
                all_of(dens.at[s - 1, pl.ds(0, rows - 1)], dens_sem.at[s - 1])
            for q in range(s):
                j = s - 1 - q
                picked = jnp.concatenate([dens[q, near[k, 0, j]] for k in range(slots)], 1)
                near_field = near_field + product(picked, khigh[j], klow[j])
            dens[s, row] = product(inc[s] - near_field, ihigh[...], ilow[...])
            if s < steps - 1:
                for m in range(1, rows):
                    dens_copy(s, m).start()
            for g in range(1, groups):
                result_copy(s, g).start()
            keep(s).start()
        for s in range(steps):
            if s < steps - 1:
                all_of(dens.at[s, pl.ds(0, rows - 1)], dens_send.at[s])
            all_of(dens.at[s, pl.ds(0, groups - 1)], res_send.at[s])
            keep(s).wait()

    for c in range(chunks):
        if half > 1:
            all_of(past[c].at[core, pl.ds(0, half - 1)], send_sem.at[c])
        chunk_pass(c).wait_send()
    if ahead > 0:

        @pl.when(group < groups - 1)
        def _():
            all_of(extra.at[core], extra_send)

        @pl.when(group > 0)
        def _():
            extra_pass().wait_send()


def solution(mesh):
    rows, groups = mesh.shape["rows"], mesh.shape["lags"]

    def shards(history, incident, kernel, near_blocks, self_inverse):
        lags, waves, block = history.shape
        steps = incident.shape[0]
        slots = near_blocks.shape[2]
        per_chunk = 2 if lags % 2 == 0 else 1
        chunks = lags // per_chunk
        half = rows // 2
        ahead = steps - 1
        f32, bf16 = jnp.float32, jnp.bfloat16
        dma = pltpu.SemaphoreType.DMA
        anywhere = pl.BlockSpec(memory_space=pl.ANY)
        return pl.pallas_call(
            functools.partial(march, rows, groups, per_chunk),
            out_shape=jax.ShapeDtypeStruct((steps, waves, block), f32),
            in_specs=[pl.BlockSpec(memory_space=pltpu.SMEM)] + [anywhere] * 4,
            out_specs=anywhere,
            scratch_shapes=[
                pltpu.VMEM((lags, slots, block, block), f32),
                pltpu.VMEM((lags, slots * block, block), bf16),
                pltpu.VMEM((lags, slots * block, block), bf16),
                pltpu.VMEM((2, half, max(ahead, 1), waves, block), f32),
                pltpu.VMEM((steps, waves, block), f32),
                pltpu.VMEM((groups, steps, waves, block), f32),
                pltpu.VMEM((steps, rows, waves, block), f32),
                pltpu.VMEM((steps, waves, block), f32),
                pltpu.VMEM((block, block), f32),
                pltpu.VMEM((block, block), bf16),
                pltpu.VMEM((block, block), bf16),
                dma((lags,)), dma((2,)), dma((chunks,)), dma((steps,)),
                dma((chunks,)), dma((chunks,)), dma((chunks,)), dma((chunks,)),
                dma, dma, dma, dma,
                dma((steps,)), dma((steps,)), dma((steps,)), dma((steps,)), dma((steps,)), dma((steps,)),
            ]
            + [pltpu.VMEM((2, half, per_chunk, waves, block), f32)] * chunks,
            compiler_params=pltpu.CompilerParams(
                collective_id=0, has_side_effects=True, vmem_limit_bytes=VMEM_LIMIT
            ),
            cost_estimate=pl.CostEstimate(
                flops=6 * steps * lags * slots * waves * block * block,
                bytes_accessed=4 * lags * slots * block * block,
                transcendentals=0,
            ),
        )(jnp.transpose(near_blocks, (2, 0, 1)), history, incident, kernel, self_inverse)

    in_specs = (
        P("lags", None, "rows"),
        P(None, None, "rows"),
        P("rows", "lags", None, None, None),
        P("rows", "lags", None),
        P("rows", None, None),
    )
    return jax.shard_map(
        shards, mesh=mesh, in_specs=in_specs, out_specs=P(None, None, "rows"), check_vma=False
    )
```

time: 104 us -> 30.1 us (0.29)
  blocking collectives: 60 us -> 0 us
  Pallas kernels: 0 us -> 28.5 us
  matrix products: 20.4 us -> 0 us
  waiting for transfers between devices: 7.84 us -> 0 us
  starting transfers between devices: 7.05 us -> 0 us
  local copies, waits for them, and re-layouts: 6.1 us -> 1.38 us
  other arithmetic: 1.82 us -> 0 us
    psum x2 -> x0, blocking collectives: 34.6 us -> none  [solve_from(): near_field = lax.psum(partial_value, 'lags')]
    pallas_call x0 -> x1, Pallas kernels: none -> 28.5 us  [shards(): pl.pallas_call(functools.partial(march, rows, groups, per_chunk), out_sha...]
    dot_general x6 -> x0, matrix products: 20.4 us -> none  [the longest x2 18.4 us: solve_from(): jnp.einsum('jkwc,jkcr->wr', picked, kernel_rows, precision=highest)]
    all_to_all x1 -> x0, blocking collectives: 15 us -> none  [fetch_and_solve(): lax.all_to_all(outgoing, 'rows', split_axis=0, concat_axis=0, tiled=True)]
    all_gather x1 -> x0, blocking collectives: 10.5 us -> none  [shards(): all_near = lax.all_gather(near_blocks, 'rows', axis=0, tiled=True)]
    all_to_all x1 -> x0, waiting for transfers between devices: 7.84 us -> none  [fetch_and_solve(): lax.all_to_all(outgoing, 'rows', split_axis=0, concat_axis=0, tiled=True)]
    all_to_all x1 -> x0, starting transfers between devices: 3.55 us -> none  [fetch_and_solve(): lax.all_to_all(outgoing, 'rows', split_axis=0, concat_axis=0, tiled=True)]
    ppermute x1 -> x0, starting transfers between devices: 3.51 us -> none  [shifted(): return lax.ppermute(block, axis, route)]
  transfers between devices with their start and end apart: 2 -> 0, of which waited for: 1 -> 0; matrix products, arithmetic and copies ran while one was open for 11% -> 0% of each run, Pallas kernels for 0% -> 0%
where the time goes in v1:
time: 30.1 us; the launch traced here: 29.9 us
  Pallas kernels  28.5 us (95%)
  local copies, waits for them, and re-layouts  1.38 us (5%)
    pallas_call x1, Pallas kernels, shards(): pl.pallas_call(functools.partial(march, rows, groups, per_chunk), out_sha...  28.5 us
    unnamed x1, local copies, waits for them, and re-layouts  1.38 us

profile of v1, /device:TPU:0, one launch (start us, length us, event | category | flops | bytes accessed | tf_op | source)
XLA Modules:
  0.0 29.9 jit_solution(12995299998190699058)
XLA Ops:
  0.0 28.5 %shard_map.55 = f32[2,16,256]{2,1,0:T(8,128)} custom-call(s32[6,1,8]{2,1,0:T(1,128)} %bitcast.1, f32[8,16,256]{2,1,0:T(8,128)} %hist.1, f32[2,16,256]{2,1,0:T(8,128)} %inc_hbm.1, f32[1,8,6,256,256]{4,3,2,1,0:T(8,128)} %ker.1, f32[1,256,256]{2,1,0:T(8,128)} %inv_hbm.1), custom_call_target="tpu_custom_call" | custom-call | flops 603979776 | bytes 12582912 | tf_op jit(solution)/shard_map/pallas_call | solution.py:285
  28.5 1.4 %copy.7 = f32[2,16,256]{2,1,0:T(8,128)} copy(f32[2,16,256]{2,1,0:T(8,128)} %shard_map.55) | data formatting | bytes 65536

commit v2 on v1

--- a/solution.py
+++ b/solution.py
@@ -32,7 +32,7 @@
     ker_sem, in_sem, own_sem, out_sem,
     send_sem, direct_sem, pass_send, pass_sem,
     extra_send, extra_sem, epass_send, epass_sem,
-    part_send, part_sem, dens_send, dens_sem, res_send, res_sem,
+    relay_send, relay_sem, part_send, part_sem, dens_send, dens_sem, res_send, res_sem,
     *past,
 ):
     lags, waves, block = hist.shape
@@ -46,6 +46,7 @@
     core = lax.rem(row, 2)
     place = lax.div(row, 2)
     partner = row + 1 - 2 * core
+    square = rows == 8
 
     def remote(src, dst, send, recv, r, g):
         return pltpu.make_async_remote_copy(
@@ -71,11 +72,12 @@
 
     barrier = pltpu.get_barrier_semaphore()
 
+    def peer(m):
+        return jnp.bitwise_xor(row, m) if square else lax.rem(row + m, rows)
+
     def greet(r, g):
         pl.semaphore_signal(barrier, inc=1, device_id=(r, g), device_id_type=MESH)
 
-    for m in range(1, rows):
-        greet(lax.rem(row + m, rows), group)
     for m in range(1, groups):
         greet(row, lax.rem(group + m, groups))
 
@@ -89,49 +91,13 @@
         for m in range(1, half):
             greet(lax.rem(row + 2 * m, rows), group + 1)
 
+    for m in range(rows - 1, 0, -1):
+        greet(peer(m), group)
+
     for load in loads:
         load.start()
     inv_load.start()
     inc_load.start()
-
-    sides = (group > 0).astype(jnp.int32) + (group < groups - 1).astype(jnp.int32)
-    pl.semaphore_wait(barrier, rows - 1 + groups - 1 + (half - 1) * sides)
-
-    def chunk_copy(c, m):
-        return remote(
-            lags_of(c), past[c].at[core, place],
-            send_sem.at[c], direct_sem.at[c], lax.rem(row + 2 * m, rows), group,
-        )
-
-    def chunk_pass(c):
-        ref = past[c].at[core]
-        return remote(ref, ref, pass_send.at[c], pass_sem.at[c], partner, group)
-
-    def extra_copy(m, g):
-        return remote(
-            hist.at[pl.ds(lags - ahead, ahead)], extra.at[core, place],
-            extra_send, extra_sem, lax.rem(row + 2 * m, rows), g,
-        )
-
-    def extra_pass():
-        ref = extra.at[core]
-        return remote(ref, ref, epass_send, epass_sem, partner, group)
-
-    for c in range(chunks):
-        for m in range(1, half):
-            chunk_copy(c, m).start()
-        if c == 0 and ahead > 0:
-
-            @pl.when(group < groups - 1)
-            def _():
-                for m in range(half):
-                    extra_copy(m, group + 1).start()
-
-    if ahead > 0:
-
-        @pl.when(group == 0)
-        def _():
-            extra[...] = jnp.zeros(extra.shape, jnp.float32)
 
     def convert(j):
         loads[j].wait()
@@ -143,10 +109,71 @@
             khigh[j, at] = high
             klow[j, at] = low
 
-    def pass_on(c):
+    early = min(0, lags)
+    for j in range(early):
+        convert(j)
+
+    sides = (group > 0).astype(jnp.int32) + (group < groups - 1).astype(jnp.int32)
+    pl.semaphore_wait(barrier, rows - 1 + groups - 1 + (half - 1) * sides)
+
+    def chunk_copy(c, m):
+        return remote(
+            lags_of(c), past[c].at[core, place],
+            send_sem.at[c], direct_sem.at[c], peer(2 * m), group,
+        )
+
+    relayed = [False for c in range(chunks)]
+
+    def chunk_relay(c):
+        first, second = (4, 2) if c % 2 == 0 else (2, 4)
+        ref = past[c].at[core, lax.div(jnp.bitwise_xor(row, first), 2)]
+        return remote(
+            ref, ref, relay_send.at[c], relay_sem.at[c], jnp.bitwise_xor(row, second), group
+        )
+
+    def straight(c):
+        return range(1, half - 1) if relayed[c] else range(half - 1, 0, -1)
+
+    def chunk_pass(c):
+        ref = past[c].at[core]
+        return remote(ref, ref, pass_send.at[c], pass_sem.at[c], partner, group)
+
+    def extra_copy(m, g):
+        return remote(
+            hist.at[pl.ds(lags - ahead, ahead)], extra.at[core, place],
+            extra_send, extra_sem, lax.rem(row + 2 * m, rows), g,
+        )
+
+    def extra_pass():
+        ref = extra.at[core]
+        return remote(ref, ref, epass_send, epass_sem, partner, group)
+
+    for c in range(chunks):
+        for m in straight(c):
+            chunk_copy(c, m).start()
+        if c == 0 and ahead > 0:
+
+            @pl.when(group < groups - 1)
+            def _():
+                for m in range(half):
+                    extra_copy(m, group + 1).start()
+
+    if ahead > 0:
+
+        @pl.when(group == 0)
+        def _():
+            extra[...] = jnp.zeros(extra.shape, jnp.float32)
+
+    def relay(c):
         own[c].wait()
         if half > 1:
-            all_of(past[c].at[core, pl.ds(0, half - 1)], direct_sem.at[c])
+            all_of(past[c].at[core, pl.ds(0, len(straight(c)))], direct_sem.at[c])
+        if relayed[c]:
+            chunk_relay(c).start()
+
+    def pass_on(c):
+        if relayed[c]:
+            chunk_relay(c).wait_recv()
         chunk_pass(c).start()
 
     def entry(h, b):
@@ -169,36 +196,43 @@
             else:
                 acc[...] += value
 
-    done = 0
-    for c in range(chunks):
-        for j in range(c * per_chunk, (c + 1) * per_chunk):
-            convert(j)
-        pass_on(c)
-        if c == min(1, chunks - 1) and ahead > 0:
+    def extra_in():
+        if ahead > 0:
 
             @pl.when(group > 0)
             def _():
                 all_of(extra.at[core], extra_sem)
                 extra_pass().start()
 
+    def extra_wait():
+        if ahead > 0:
+
+            @pl.when(group > 0)
+            def _():
+                extra_pass().wait_recv()
+
+    turn = early
+    inv_at = max(chunks - 2, 0)
+    for c in range(chunks):
+        upto = min(lags, max(turn, 0 + (c + 1) * per_chunk))
+        for j in range(turn, upto):
+            convert(j)
+        turn = upto
+        relay(c)
+        if not relayed[c]:
+            pass_on(c)
+        if c >= 1 and relayed[c - 1]:
+            pass_on(c - 1)
+        if c == chunks // 2 - 1:
+            extra_in()
+        if c == inv_at:
+            inv_load.wait()
+            ihigh[...], ilow[...] = split(inv[...])
         if c >= 2:
-            if done == 0 and ahead > 0:
-
-                @pl.when(group > 0)
-                def _():
-                    extra_pass().wait_recv()
-
-            multiply(done)
-            done += 1
-    if done == 0 and ahead > 0:
-
-        @pl.when(group > 0)
-        def _():
-            extra_pass().wait_recv()
-
-    inv_load.wait()
-    ihigh[...], ilow[...] = split(inv[...])
-    for c in range(done, chunks):
+            if c == 2:
+                extra_wait()
+            multiply(c - 2)
+    for c in range(max(chunks - 2, 0), chunks):
         multiply(c)
 
     def part_copy(s, to):
@@ -210,7 +244,7 @@
 
     def dens_copy(s, m):
         ref = dens.at[s, row]
-        return remote(ref, ref, dens_send.at[s], dens_sem.at[s], lax.rem(row + m, rows), group)
+        return remote(ref, ref, dens_send.at[s], dens_sem.at[s], peer(m), group)
 
     inc_load.wait()
 
@@ -242,7 +276,7 @@
                 near_field = near_field + product(picked, khigh[j], klow[j])
             dens[s, row] = product(inc[s] - near_field, ihigh[...], ilow[...])
             if s < steps - 1:
-                for m in range(1, rows):
+                for m in range(rows - 1, 0, -1):
                     dens_copy(s, m).start()
             for g in range(1, groups):
                 result_copy(s, g).start()
@@ -255,7 +289,9 @@
 
     for c in range(chunks):
         if half > 1:
-            all_of(past[c].at[core, pl.ds(0, half - 1)], send_sem.at[c])
+            all_of(past[c].at[core, pl.ds(0, len(straight(c)))], send_sem.at[c])
+        if relayed[c]:
+            chunk_relay(c).wait_send()
         chunk_pass(c).wait_send()
     if ahead > 0:
 
@@ -301,7 +337,7 @@
                 pltpu.VMEM((block, block), bf16),
                 dma((lags,)), dma((2,)), dma((chunks,)), dma((steps,)),
                 dma((chunks,)), dma((chunks,)), dma((chunks,)), dma((chunks,)),
-                dma, dma, dma, dma,
+                dma, dma, dma, dma, dma((chunks,)), dma((chunks,)),
                 dma((steps,)), dma((steps,)), dma((steps,)), dma((steps,)), dma((steps,)), dma((steps,)),
             ]
             + [pltpu.VMEM((2, half, per_chunk, waves, block), f32)] * chunks,

time: 30.1 us -> 29.8 us (0.990)
    pallas_call x1, Pallas kernels: 28.5 us -> 28.2 us  [shards(): pl.pallas_call(functools.partial(march, rows, groups, per_chunk), out_sha...]
where the time goes in v2:
time: 29.8 us; the launch traced here: 29.6 us
  Pallas kernels  28.2 us (95%)
  local copies, waits for them, and re-layouts  1.38 us (5%)
    pallas_call x1, Pallas kernels, shards(): pl.pallas_call(functools.partial(march, rows, groups, per_chunk), out_sha...  28.2 us
    unnamed x1, local copies, waits for them, and re-layouts  1.38 us

profile of v2, /device:TPU:0, one launch (start us, length us, event | category | flops | bytes accessed | tf_op | source)
XLA Modules:
  0.0 29.6 jit_solution(10317278172843757574)
XLA Ops:
  0.0 28.2 %shard_map.55 = f32[2,16,256]{2,1,0:T(8,128)} custom-call(s32[6,1,8]{2,1,0:T(1,128)} %bitcast.1, f32[8,16,256]{2,1,0:T(8,128)} %hist.1, f32[2,16,256]{2,1,0:T(8,128)} %inc_hbm.1, f32[1,8,6,256,256]{4,3,2,1,0:T(8,128)} %ker.1, f32[1,256,256]{2,1,0:T(8,128)} %inv_hbm.1), custom_call_target="tpu_custom_call" | custom-call | flops 603979776 | bytes 12582912 | tf_op jit(solution)/shard_map/pallas_call | solution.py:321
  28.2 1.4 %copy.7 = f32[2,16,256]{2,1,0:T(8,128)} copy(f32[2,16,256]{2,1,0:T(8,128)} %shard_map.55) | data formatting | bytes 65536

commit v3 on v2

--- a/solution.py
+++ b/solution.py
@@ -113,12 +113,15 @@
     for j in range(early):
         convert(j)
 
+    for copy in own:
+        copy.wait()
+
     sides = (group > 0).astype(jnp.int32) + (group < groups - 1).astype(jnp.int32)
     pl.semaphore_wait(barrier, rows - 1 + groups - 1 + (half - 1) * sides)
 
     def chunk_copy(c, m):
         return remote(
-            lags_of(c), past[c].at[core, place],
+            past[c].at[core, place], past[c].at[core, place],
             send_sem.at[c], direct_sem.at[c], peer(2 * m), group,
         )
 
@@ -165,7 +168,6 @@
             extra[...] = jnp.zeros(extra.shape, jnp.float32)
 
     def relay(c):
-        own[c].wait()
         if half > 1:
             all_of(past[c].at[core, pl.ds(0, len(straight(c)))], direct_sem.at[c])
         if relayed[c]:

time: 29.8 us -> 29.6 us (level)
  no operation moved by 1% of the time
where the time goes in v3:
time: 29.6 us; the launch traced here: 29.4 us
  Pallas kernels  28 us (95%)
  local copies, waits for them, and re-layouts  1.38 us (5%)
    pallas_call x1, Pallas kernels, shards(): pl.pallas_call(functools.partial(march, rows, groups, per_chunk), out_sha...  28 us
    unnamed x1, local copies, waits for them, and re-layouts  1.38 us

profile of v3, /device:TPU:0, one launch (start us, length us, event | category | flops | bytes accessed | tf_op | source)
XLA Modules:
  0.0 29.4 jit_solution(9943295262139370450)
XLA Ops:
  0.0 28.0 %shard_map.55 = f32[2,16,256]{2,1,0:T(8,128)} custom-call(s32[6,1,8]{2,1,0:T(1,128)} %bitcast.1, f32[8,16,256]{2,1,0:T(8,128)} %hist.1, f32[2,16,256]{2,1,0:T(8,128)} %inc_hbm.1, f32[1,8,6,256,256]{4,3,2,1,0:T(8,128)} %ker.1, f32[1,256,256]{2,1,0:T(8,128)} %inv_hbm.1), custom_call_target="tpu_custom_call" | custom-call | flops 603979776 | bytes 12582912 | tf_op jit(solution)/shard_map/pallas_call | solution.py:323
  28.0 1.4 %copy.7 = f32[2,16,256]{2,1,0:T(8,128)} copy(f32[2,16,256]{2,1,0:T(8,128)} %shard_map.55) | data formatting | bytes 65536
